TPU v7x, 512 devices: a whole 4x4x16 slice. The times are simulated.
512 devices in a mesh: tok: 128 (over z, x, core), grp: 4 (over y).
Axes of the slice: x: 4, y: 4, z: 16, core: 2. Of those that a mesh axis runs over, the one named last changes fastest.
Arguments:
- queries: bfloat16 [24576, 2048], P('tok', 'grp'), may hold values from -72 to 72
- new_keys: bfloat16 [24576, 2048], P('tok', 'grp'), may hold values from -8 to 8
- new_values: bfloat16 [24576, 2048], P('tok', 'grp'), may hold values from -6 to 6
- residual: bfloat16 [24576, 2048], P('tok', 'grp'), may hold values from -6 to 6
- w_out: bfloat16 [2048, 2048], P('grp'), may hold values from -0.125 to 0.125
- leaf_keys: bfloat16 [128, 512, 2048], P('tok', None, 'grp'), may hold values from -6 to 6
- leaf_values: bfloat16 [128, 512, 2048], P('tok', None, 'grp'), may hold values from -6 to 6
- upper_keys: bfloat16 [6, 1024, 2048], P(None, 'tok', 'grp'), may hold values from -8 to 8
- upper_values: bfloat16 [6, 1024, 2048], P(None, 'tok', 'grp'), may hold values from -6 to 6
- req_len: int32 [128], replicated, may hold values from 48 to 192, as said below
- leaf_mid: int32 [128], replicated, may hold values from 0 to 3
- mid_root: int32 [4], replicated, may hold values from 0 to 1, as said below
- upper_len: int32 [6], replicated, may hold values from 256 to 1024, as said below
- leaf_len: int32 [128], replicated, may hold values from 128 to 512, as said below
Outputs:
- hidden_out: bfloat16 [24576, 2048], P('tok', 'grp')
Inputs may be any that keep to these rules, and one draw needn't show every extreme that they name: `req_len`: some request has exactly 192 new tokens. `mid_root`: each root is the parent of 2 mids. `upper_len`: the first 2 entries are roots and equal 1024. `leaf_len`: some leaf has exactly 512 positions.
All inputs are finite; a program needn't handle non-finite values.
Results may differ from a plain program's by a relative error of at most 0.008.
Values may be sent and summed in bfloat16 or wider, within the bound.
A program may use at most 64 MiB of HBM per device.

v0:
```python
import math

import jax
import jax.numpy as jnp
from jax import lax
from jax.sharding import PartitionSpec as P

HEAD_DIM = 128


NEG_FILL = -1e30


def partial_attention(query_rows, key_rows, values, allowed, head_count):
    head_width = query_rows.shape[1] // head_count
    query_heads = query_rows.reshape(query_rows.shape[0], head_count, head_width)
    key_heads = key_rows.reshape(key_rows.shape[0], head_count, head_width)
    value_heads = values.reshape(values.shape[0], head_count, head_width)
    scores = jnp.einsum(
        "qhd,khd->hqk", query_heads, key_heads, preferred_element_type=jnp.float32
    ) * head_width ** (-0.5)
    scores = jnp.where(allowed[None], scores, NEG_FILL)
    row_max = jnp.max(scores, axis=2)
    exp_scores = jnp.where(allowed[None], jnp.exp(scores - row_max[:, :, None]), 0.0)
    row_total = jnp.sum(exp_scores, axis=2)
    weighted = jnp.einsum(
        "hqk,khd->hqd",
        exp_scores.astype(jnp.bfloat16),
        value_heads,
        preferred_element_type=jnp.float32,
    )
    return (row_max, row_total, weighted)


def combine(earlier, latter):
    new_max = jnp.maximum(earlier[0], latter[0])
    earlier_scale = jnp.exp(earlier[0] - new_max)
    latter_scale = jnp.exp(latter[0] - new_max)
    return (
        new_max,
        earlier[1] * earlier_scale + latter[1] * latter_scale,
        earlier[2] * earlier_scale[:, :, None] + latter[2] * latter_scale[:, :, None],
    )


def node_attention(carry, query_rows, node_keys, node_values, node_len, head_count):
    node_rows = node_keys.shape[0]
    block = math.gcd(node_rows, 512)
    row_count = query_rows.shape[0]
    for start in range(0, node_rows, block):
        positions = start + jnp.arange(block, dtype=jnp.int32)
        allowed = jnp.broadcast_to((positions < node_len)[None, :], (row_count, block))
        piece_part = partial_attention(
            query_rows,
            node_keys[start : start + block],
            node_values[start : start + block],
            allowed,
            head_count,
        )
        carry = combine(carry, piece_part)
    return carry


def shards(
    queries,
    new_keys,
    new_values,
    residual,
    w_out,
    leaf_keys,
    leaf_values,
    upper_keys,
    upper_values,
    req_len,
    leaf_mid,
    mid_root,
    upper_len,
    leaf_len,
):
    dev_count = lax.axis_size("tok")
    my_index = lax.axis_index("tok")
    row_count = queries.shape[0]
    col_count = queries.shape[1]
    head_count = col_count // HEAD_DIM
    mid_count = mid_root.shape[0]
    node_count = upper_len.shape[0]
    root_count = node_count - mid_count
    owned = (jnp.arange(dev_count, dtype=jnp.int32) == my_index).astype(jnp.int32)
    my_length = jnp.sum(owned * req_len)
    my_mid = jnp.sum(owned * leaf_mid)
    my_leaf_len = jnp.sum(owned * leaf_len)
    my_root = jnp.sum((jnp.arange(mid_count) == my_mid).astype(jnp.int32) * mid_root)
    node_ids = jnp.arange(node_count)
    root_len = jnp.sum((node_ids == my_root).astype(jnp.int32) * upper_len)
    mid_len = jnp.sum((node_ids == root_count + my_mid).astype(jnp.int32) * upper_len)
    position = jnp.arange(row_count, dtype=jnp.int32)
    is_live = position < my_length
    leaf_count = leaf_keys.shape[1]
    local_keys = jnp.concatenate([leaf_keys[0], new_keys], axis=0)
    local_values = jnp.concatenate([leaf_values[0], new_values], axis=0)
    leaf_allowed = jnp.broadcast_to(
        (jnp.arange(leaf_count) < my_leaf_len)[None, :], (row_count, leaf_count)
    )
    new_allowed = (position[None, :] <= position[:, None]) & is_live[None, :]
    local_part = partial_attention(
        queries,
        local_keys,
        local_values,
        jnp.concatenate([leaf_allowed, new_allowed], axis=1),
        head_count,
    )
    gathered_keys, gathered_values = (
        lax.all_gather(upper_keys, "tok", axis=1, tiled=True),
        lax.all_gather(upper_values, "tok", axis=1, tiled=True),
    )
    merged = node_attention(
        local_part, queries, gathered_keys[my_root], gathered_values[my_root], root_len, head_count
    )
    merged = node_attention(
        merged,
        queries,
        gathered_keys[root_count + my_mid],
        gathered_values[root_count + my_mid],
        mid_len,
        head_count,
    )
    attended = (merged[2] / merged[1][:, :, None]).transpose(1, 0, 2).reshape(row_count, col_count)
    attention = jnp.where(is_live[:, None], attended, 0.0).astype(jnp.bfloat16)
    projected = jnp.dot(attention, w_out, preferred_element_type=jnp.float32)
    mixed = lax.psum_scatter(
        projected.astype(jnp.bfloat16), "grp", scatter_dimension=1, tiled=True
    ).astype(jnp.float32)
    return (residual.astype(jnp.float32) + mixed).astype(jnp.bfloat16)


def solution(mesh):
    in_specs = (
        P("tok", "grp"),
        P("tok", "grp"),
        P("tok", "grp"),
        P("tok", "grp"),
        P("grp", None),
        P("tok", None, "grp"),
        P("tok", None, "grp"),
        P(None, "tok", "grp"),
        P(None, "tok", "grp"),
        P(),
        P(),
        P(),
        P(),
        P(),
    )
    out_specs = P("tok", "grp")
    return jax.shard_map(shards, mesh=mesh, in_specs=in_specs, out_specs=out_specs, check_vma=False)
```

profile of v0, /device:TPU:1, one launch (start us, length us, event | category | flops | bytes accessed | tf_op | source)
XLA Modules:
  0.0 358.0 jit_solution(14174177319630224316)
XLA Ops:
  6.5 0.0 all-gather.5.cloned.1.call-start
  6.5 0.7 all-gather.5.cloned.1.call-update
  7.3 0.0 all-gather.3.cloned.1.call-start
  7.3 0.7 all-gather.3.cloned.1.call-update
  8.0 0.0 reduce-scatter.2.cloned.1.call-start
  8.1 1.3 select_reduce_fusion
  10.7 2.0 fusion.91
  13.9 1.3 copy.42
  15.1 0.0 copy-start.16
  15.1 0.0 copy-start.17
  15.2 1.0 copy.43
  16.2 0.0 copy-done.8
  16.2 0.2 copy.46
  16.4 1.0 copy.47
  18.0 0.6 iota_compare_fusion.3
  18.6 1.2 fusion.92
  19.9 0.6 iota_compare_fusion.1
  20.5 0.6 fusion.89
  21.0 0.7 fusion.90
  21.7 0.7 iota_compare_fusion.2
  22.4 0.6 select_reduce_fusion.2
  23.0 0.6 iota_compare_fusion.4
  23.7 0.1 pad_add_fusion
  23.8 1.0 copy_bitcast_fusion.1
  24.7 1.6 copy_bitcast_fusion
  26.4 0.7 fusion
  27.1 1.4 copy-done.2
  28.5 0.9 fusion.1
  29.3 129.4 %all-gather.5.cloned.1.call-done = bf16[6,1024,512]{2,1,0:T(8,128)(2,1)} async-done(((bf16[6,8,512]{2,1,0:T(8,128)(2,1)}), bf16[6,1024,512]{2,1,0:T(8,128)(2,1)}) %all-gather.5.cloned.1.call-update) | async-done | bytes 6291472 | tf_op jit(solution)/shard_map/all_gather | solution.py:114
  158.7 2.7 constant_dynamic-slice_fusion.4
  161.4 2.1 copy.83
  163.5 135.8 %all-gather.3.cloned.1.call-done = bf16[6,1024,512]{2,1,0:T(8,128)(2,1)} async-done(((bf16[6,8,512]{2,1,0:T(8,128)(2,1)}), bf16[6,1024,512]{2,1,0:T(8,128)(2,1)}) %all-gather.3.cloned.1.call-update) | async-done | bytes 6291472 | tf_op jit(solution)/shard_map/all_gather | solution.py:113
  299.2 2.9 constant_dynamic-slice_fusion.3
  302.1 2.1 copy.81
  304.2 2.0 copy.84
  306.3 2.1 copy.78
  308.3 2.0 copy.75
  310.4 2.0 copy.77
  312.4 1.1 copy.79
  313.5 1.1 copy.85
  314.6 1.5 bitcast_reduce_fusion.1
  316.1 0.4 bitcast_reduce_fusion
  316.5 0.6 fusion.17
  317.1 0.6 fusion.15
  317.6 0.4 bitcast_reduce_fusion.2
  318.1 0.6 fusion.13
  318.6 0.0 copy-done.4
  318.7 0.4 bitcast_reduce_fusion.3
  319.1 0.6 fusion.11
  319.7 0.5 fusion.22
  320.2 0.0 copy-start.14
  320.2 0.5 copy-done.12
  320.7 0.5 fusion.24
  321.2 0.7 copy-done.3
  322.0 1.0 fusion.31
  322.9 0.1 copy-done.7
  323.0 0.5 fusion.32
  323.6 0.5 copy-done.10
  324.0 0.5 fusion.30
  324.6 0.0 copy-start.15
  324.6 1.5 convolution_convert_fusion
  326.1 0.0 reduce-scatter.2.cloned.1.call-update
  326.1 23.6 %reduce-scatter.2.cloned.1.call-done = bf16[192,512]{1,0:T(8,128)(2,1)} async-done(((bf16[192,2048]{1,0:T(8,128)(2,1)}), bf16[192,512]{1,0:T(8,128)(2,1)}) %reduce-scatter.2.cloned.1.call-update) | async-done | bytes 196624 | tf_op jit(solution)/shard_map/reduce_scatter | solution.py:130
  349.8 1.7 add_convert_fusion
  (28 shorter events, 0.1 us)
Async XLA Ops:
  6.5 318.0 %copy-start = (bf16[512,2048]{1,0:T(8,128)(2,1)S(1)}, bf16[512,2048]{1,0:T(8,128)(2,1)}, u32[]{:S(2)}) copy-start(bf16[512,2048]{1,0:T(8,128)(2,1)} %param.18) | copy-start | bytes 6291460
  6.5 9.7 %copy-start.8 = (bf16[1,512,512]{2,1,0:T(8,128)(2,1)S(1)}, bf16[1,512,512]{2,1,0:T(8,128)(2,1)}, u32[]{:S(2)}) copy-start(bf16[1,512,512]{2,1,0:T(8,128)(2,1)} %param.20) | copy-start | bytes 1572868
  6.5 152.2 %all-gather.5.cloned.1.call-start = ((), (), s32[]{:S(2)}) async-start(), calls=%async_computation.2 | async-start | bytes 6340608 | tf_op jit(solution)/shard_map/all_gather | solution.py:114
  7.3 292.0 %all-gather.3.cloned.1.call-start = ((), (), s32[]{:S(2)}) async-start(), calls=%async_computation.1 | async-start | bytes 6340608 | tf_op jit(solution)/shard_map/all_gather | solution.py:113
  8.0 341.8 %reduce-scatter.2.cloned.1.call-start = ((), (), s32[]{:S(2)}) async-start(), calls=%async_computation.3 | async-start | bytes 983040 | tf_op jit(solution)/shard_map/reduce_scatter | solution.py:130
  15.1 3.5 copy-start.16
  15.1 7.2 %copy-start.17 = (s32[128]{0:T(128)S(1)}, s32[128]{0:T(128)}, u32[]{:S(2)}) copy-start(s32[128]{0:T(128)} %param.23) | copy-start | bytes 1540
  16.2 10.2 %copy-start.1 = (bf16[192,512]{1,0:T(8,128)(2,1)S(1)}, bf16[192,512]{1,0:T(8,128)(2,1)}, u32[]{:S(2)}) copy-start(bf16[192,512]{1,0:T(8,128)(2,1)} %param.14) | copy-start | bytes 589828
  16.4 10.0 %copy-start.13 = (bf16[512,4,128]{2,0,1:T(8,128)(2,1)S(1)}, bf16[512,4,128]{2,0,1:T(8,128)(2,1)}, u32[]{:S(2)}) copy-start(bf16[512,4,128]{2,0,1:T(8,128)(2,1)} %copy.43) | copy-start | bytes 1572868
  27.1 1.4 copy-start.2
  313.5 2.6 copy-start.6
  316.5 1.1 copy-start.5
  317.6 1.0 copy-start.4
  318.7 1.1 copy-start.11
  319.7 1.1 copy-start.12
  319.7 1.5 copy-start.9
  320.2 1.7 copy-start.3
  320.2 1.7 copy-start.14
  322.0 1.0 copy-start.7
  323.0 1.0 copy-start.10
  324.6 25.2 %copy-start.15 = (bf16[192,512]{1,0:T(8,128)(2,1)S(1)}, bf16[192,512]{1,0:T(8,128)(2,1)}, u32[]{:S(2)}) copy-start(bf16[192,512]{1,0:T(8,128)(2,1)} %param.17) | copy-start | bytes 589828
Sparse Core Ops, SparseCore 0:
  10.4 148.3 all-gather.4
  161.7 137.4 all-gather.2
  326.2 23.4 reduce-scatter.1
where the time goes:
time: 359 us; the launch traced here: 358 us
  waiting for transfers between devices  290 us (81%)
  local copies, waits for them, and re-layouts  29.5 us (8%)
  between operations  16.5 us (5%)
  other arithmetic  13.7 us (4%)
  matrix products  8 us (2%)
    all_gather x1, waiting for transfers between devices, shards(): lax.all_gather(upper_keys, 'tok', axis=1, tiled=True)  136 us
    all_gather x1, waiting for transfers between devices, shards(): lax.all_gather(upper_values, 'tok', axis=1, tiled=True)  129 us
    reduce_scatter x1, waiting for transfers between devices, shards(): lax.psum_scatter(projected.astype(jnp.bfloat16), 'grp', scatter_dimension...  23.6 us
    unnamed x46, local copies, waits for them, and re-layouts  19.2 us
  transfers between devices with their start and end apart: 3, of which 3 were waited for; matrix products, arithmetic and copies ran while one was open for 6% of the time, Pallas kernels for 0%

commit v1 on v0

v1 whole, which is shorter than its diff:
```python
import functools

import jax
import jax.numpy as jnp
from jax import lax
from jax.experimental import pallas as pl
from jax.experimental.pallas import tpu as pltpu
from jax.sharding import PartitionSpec as P

HEAD_DIM = 128
NEG_FILL = -1e30
LOG2E = 1.4426950408889634
CHIPS_X = 4
CORES = 2
MESH = pl.DeviceIdType.MESH


def dot_nt(a, b):
    return lax.dot_general(a, b, (((1,), (1,)), ((), ())), preferred_element_type=jnp.float32)


def wait_bytes(view, sem):
    pltpu.make_async_copy(view, view, sem).wait()


def col_to_row(col):
    pieces = []
    for start in range(0, col.shape[0], 128):
        piece = col[start : start + 128]
        n = piece.shape[0]
        diag = lax.broadcasted_iota(jnp.int32, (n, 128), 0) == lax.broadcasted_iota(
            jnp.int32, (n, 128), 1
        )
        spread = jnp.broadcast_to(piece, (n, 128))
        pieces.append(jnp.sum(jnp.where(diag, spread, 0.0), axis=0, keepdims=True))
    return jnp.concatenate(pieces, axis=1)


def row_to_col(row, n_rows):
    pieces = []
    for start in range(0, n_rows, 128):
        n = min(128, n_rows - start)
        diag = lax.broadcasted_iota(jnp.int32, (n, 128), 0) == lax.broadcasted_iota(
            jnp.int32, (n, 128), 1
        )
        spread = jnp.broadcast_to(row[:, start : start + 128], (n, 128))
        pieces.append(jnp.sum(jnp.where(diag, spread, 0.0), axis=1, keepdims=True))
    return jnp.concatenate(pieces, axis=0)


def softmax_part(parts):
    scale = HEAD_DIM ** (-0.5) * LOG2E
    top = functools.reduce(
        jnp.maximum, [jnp.max(s, axis=1, keepdims=True) for s, _ in parts]
    )
    total, weighted = 0.0, 0.0
    for s, v in parts:
        exps = jnp.exp2((s - top) * scale)
        total = total + jnp.sum(exps, axis=1, keepdims=True)
        weighted = weighted + jnp.dot(
            exps.astype(jnp.bfloat16), v, preferred_element_type=jnp.float32
        )
    return weighted / total, top * scale + jnp.log(total) * LOG2E


def kernel(
    nx,
    nz,
    ny,
    heads,
    roots,
    req_len,
    leaf_mid,
    mid_root,
    upper_len,
    leaf_len,
    uk,
    uv,
    q_hbm,
    nk_hbm,
    nv_hbm,
    res_hbm,
    w_hbm,
    lk_hbm,
    lv_hbm,
    out,
    *scratch,
):
    kv = scratch[:heads]
    (
        up,
        up_other,
        qx,
        lk,
        lv,
        nk,
        nv,
        res,
        w,
        leaf_o,
        leaf_lse,
        o_send,
        o_recv,
        s_send,
        s_recv,
        at,
        acc,
        in_sem,
        pre_sem,
        ring_send,
        ring_recv,
        sib_send,
        sib_recv,
        q_sem,
        w_sem,
        wf_sem,
        o_sem_s,
        o_sem_r,
        s_sem_s,
        s_sem_r,
        y_sem_s,
        y_sem_r,
    ) = scratch[heads:]
    nodes = kv[0].shape[2]
    rows = qx.shape[1]
    width = heads * HEAD_DIM
    half_rows = width // CORES
    tok, y = lax.axis_index("tok"), lax.axis_index("grp")
    c = lax.rem(tok, CORES)
    x = lax.rem(lax.div(tok, CORES), nx)
    z = lax.div(tok, CORES * nx)

    def dev(z_, x_, c_, y_):
        return ((z_ * nx + x_) * CORES + c_, y_)

    sibling = dev(z, x, 1 - c, y)
    right = dev(lax.rem(z + 1, nz), x, c, y)
    left = dev(lax.rem(z + nz - 1, nz), x, c, y)

    def x_mate(k):
        return lax.rem(x + k, nx)

    def y_mate(k):
        return lax.rem(y + k, ny)

    loads = [
        (uk, up.at[0]),
        (uv, up.at[1]),
        (q_hbm, qx.at[x]),
        (lk_hbm, lk),
        (lv_hbm, lv),
        (nk_hbm, nk),
        (nv_hbm, nv),
        (res_hbm, res),
        (w_hbm.at[:, pl.ds(pl.multiple_of(y * width, width), width)], w.at[y]),
    ]
    loads = [pltpu.make_async_copy(a, b, in_sem.at[i]) for i, (a, b) in enumerate(loads)]
    for load in loads:
        load.start()

    partners = [sibling, right, left]
    partners += [dev(z, x_mate(k), c, y) for k in range(1, nx)]
    partners += [dev(z, x, c, y_mate(k)) for k in range(1, ny)]
    barrier = pltpu.get_barrier_semaphore()
    for partner in partners:
        pl.semaphore_signal(barrier, inc=1, device_id=partner, device_id_type=MESH)
    pl.semaphore_wait(barrier, len(partners))

    def send(src, dst, send_sem, recv_sem, device):
        pltpu.make_async_remote_copy(
            src_ref=src,
            dst_ref=dst,
            send_sem=send_sem,
            recv_sem=recv_sem,
            device_id=device,
            device_id_type=MESH,
        ).start()

    loads[0].wait()
    loads[1].wait()
    send(up.at[1 - c], up_other, pre_sem.at[0], pre_sem.at[1], sibling)
    for k in range(1, nx):
        send(q_hbm, qx.at[x], q_sem.at[0], q_sem.at[1], dev(z, x_mate(k), c, y))
    my_half = pl.ds(pl.multiple_of(c * half_rows, half_rows), half_rows)
    for k in range(1, ny):
        to = y_mate(k)
        send(
            w_hbm.at[my_half, pl.ds(pl.multiple_of(to * width, width), width)],
            w.at[y, my_half],
            w_sem.at[0],
            w_sem.at[1],
            dev(z, x, c, to),
        )
    wait_bytes(up_other, pre_sem.at[1])
    mine = up[c].astype(jnp.float32).reshape(nodes, 8, width)
    other = up_other[...].astype(jnp.float32).reshape(nodes, 8, width)
    first = jnp.where(c == 0, mine, other)
    second = jnp.where(c == 0, other, mine)
    block = jnp.concatenate([first, second], axis=1).astype(jnp.bfloat16)
    for h in range(heads):
        kv[h][c, z] = block[:, :, h * HEAD_DIM : (h + 1) * HEAD_DIM]

    steps = nz // 2
    cut = nodes // 2

    def ring_view(h, direction, step):
        slot = lax.rem(z + (nz - step if direction == 0 else step), nz)
        view = kv[h].at[c, slot]
        return view

    def ring_part(h, direction, step, hop):
        view = ring_view(h, direction, step)
        if hop == steps:
            view = view.at[pl.ds(0, cut)] if direction == 0 else view.at[pl.ds(cut, nodes - cut)]
        return view

    def ring_start(h, direction, step):
        view = ring_part(h, direction, step, step + 1)
        send(
            view,
            view,
            ring_send.at[h],
            ring_recv.at[h, direction, step],
            right if direction == 0 else left,
        )

    def ring_wait(h, direction, step):
        wait_bytes(
            ring_part(h, direction, step + 1, step + 1), ring_recv.at[h, direction, step]
        )

    def share(h, view):
        send(view, view, sib_send.at[h], sib_recv.at[h], sibling)

    for h in range(heads):
        for direction in range(2):
            ring_start(h, direction, 0)
    for h in range(heads):
        share(h, kv[h].at[c, z])

    me = tok
    position = lax.broadcasted_iota(jnp.int32, (rows, 1), 0)

    def leaf_part(h):
        cols = slice(h * HEAD_DIM, (h + 1) * HEAD_DIM)
        query = qx[x, :, cols]
        leaf_scores = dot_nt(query, lk[:, cols])
        at_pos = lax.broadcasted_iota(jnp.int32, leaf_scores.shape, 1)
        leaf_scores = jnp.where(at_pos < leaf_len[me], leaf_scores, NEG_FILL)
        new_scores = dot_nt(query, nk[:, cols])
        key_pos = lax.broadcasted_iota(jnp.int32, new_scores.shape, 1)
        query_pos = lax.broadcasted_iota(jnp.int32, new_scores.shape, 0)
        allowed = (key_pos <= query_pos) & (key_pos < req_len[me])
        new_scores = jnp.where(allowed, new_scores, NEG_FILL)
        o, lse = softmax_part([(leaf_scores, lv[:, cols]), (new_scores, nv[:, cols])])
        leaf_o[h] = o
        leaf_lse[h] = jnp.broadcast_to(lse, (rows, HEAD_DIM))

    for step in range(steps - 1):
        for h in range(heads):
            for direction in range(2):
                ring_wait(h, direction, step)
                ring_start(h, direction, step + 1)
                share(h, ring_view(h, direction, step + 1))
        if step == 0:
            for load in loads[2:7]:
                load.wait()
            for h in range(max(0, heads - steps + 1)):
                leaf_part(h)
        h = step + max(0, heads - steps + 1)
        if h < heads:
            leaf_part(h)
    for h in range(heads):
        for direction in range(2):
            ring_wait(h, direction, steps - 1)
        share(h, ring_view(h, 0, steps))

    wait_bytes(w.at[pl.ds(0, ny - 1), pl.ds(0, half_rows)], w_sem.at[1])
    for k in range(1, ny):
        view = w.at[y_mate(k), my_half]
        send(view, view, wf_sem.at[0], wf_sem.at[1], sibling)
    wait_bytes(qx.at[pl.ds(0, nx - 1)], q_sem.at[1])

    keys = nz * 16

    def upper_part(h, j):
        request = (z * nx + j) * CORES + c
        mid = leaf_mid[request]
        root = mid_root[mid]
        query = qx[j, :, h * HEAD_DIM : (h + 1) * HEAD_DIM]
        root_scores = dot_nt(query, kv[h][0, :, root].reshape(keys, HEAD_DIM))
        mid_scores = dot_nt(query, kv[h][0, :, roots + mid].reshape(keys, HEAD_DIM))
        key = lax.broadcasted_iota(jnp.int32, mid_scores.shape, 1)
        key_pos = (key >> 4) * (nx * 16) + (key & 15) + x * 16
        root_scores = jnp.where(key_pos < upper_len[root], root_scores, NEG_FILL)
        mid_scores = jnp.where(key_pos < upper_len[roots + mid], mid_scores, NEG_FILL)
        o, lse = softmax_part(
            [
                (root_scores, kv[h][1, :, root].reshape(keys, HEAD_DIM)),
                (mid_scores, kv[h][1, :, roots + mid].reshape(keys, HEAD_DIM)),
            ]
        )
        row = col_to_row(lse)
        return o.astype(jnp.bfloat16), jnp.broadcast_to(row, (8, row.shape[1]))

    def upper_head(h):
        wait_bytes(kv[h].at[1 - c], sib_recv.at[h])

        @pl.loop(1, nx)
        def _(k):
            j = lax.rem(x + k, nx)
            o, lse = upper_part(h, j)
            o_send[h, j] = o
            s_send[h, j] = lse
            to = dev(z, j, c, y)
            send(s_send.at[h, j], s_recv.at[h, x], s_sem_s.at[h], s_sem_r.at[h], to)
            send(o_send.at[h, j], o_recv.at[h, x], o_sem_s.at[h], o_sem_r.at[h], to)

        o, lse = upper_part(h, x)
        o_recv[h, x] = o
        s_recv[h, x] = lse

    def merge_head(h):
        wait_bytes(s_recv.at[h, pl.ds(0, nx - 1)], s_sem_r.at[h])
        wait_bytes(o_recv.at[h, pl.ds(0, nx - 1)], o_sem_r.at[h])
        sums = [row_to_col(s_recv[h, i, 0:1, :], rows) for i in range(nx)]
        sums.append(leaf_lse[h][:, 0:1])
        top = functools.reduce(jnp.maximum, sums)
        total, weighted = 0.0, 0.0
        for i in range(nx + 1):
            weight = jnp.exp2(sums[i] - top)
            part = o_recv[h, i].astype(jnp.float32) if i < nx else leaf_o[h]
            total = total + weight
            weighted = weighted + weight * part
        attended = jnp.where(position < req_len[me], weighted / total, 0.0)
        at[h, y] = attended.astype(jnp.bfloat16)
        for k in range(1, ny):
            view = at.at[h, y]
            send(view, view, y_sem_s.at[h], y_sem_r.at[h], dev(z, x, c, y_mate(k)))

    def project_head(h):
        if h == 0:
            loads[8].wait()
            wait_bytes(w.at[pl.ds(0, ny - 1), pl.ds(0, half_rows)], wf_sem.at[1])
        wait_bytes(at.at[h, pl.ds(0, ny - 1)], y_sem_r.at[h])
        total = res[...].astype(jnp.float32) if h == 0 else acc[...]
        for i in range(ny):
            total = total + jnp.dot(
                at[h, i],
                w[i, h * HEAD_DIM : (h + 1) * HEAD_DIM, :],
                preferred_element_type=jnp.float32,
            )
        if h < heads - 1:
            acc[...] = total
        else:
            out[...] = total.astype(out.dtype)

    loads[7].wait()
    for i in range(heads + 2):
        if i < heads:
            upper_head(i)
        if 1 <= i <= heads:
            merge_head(i - 1)
        if i >= 2:
            project_head(i - 2)

    wait_bytes(up_other, pre_sem.at[0])
    wait_bytes(qx.at[pl.ds(0, nx - 1)], q_sem.at[0])
    wait_bytes(w.at[pl.ds(0, ny - 1), pl.ds(0, half_rows)], w_sem.at[0])
    wait_bytes(w.at[pl.ds(0, ny - 1), pl.ds(0, half_rows)], wf_sem.at[0])
    for h in range(heads):
        wait_bytes(kv[h].at[0, pl.ds(0, nz - 1)], ring_send.at[h])
        wait_bytes(kv[h].at[0], sib_send.at[h])
        wait_bytes(s_recv.at[h, pl.ds(0, nx - 1)], s_sem_s.at[h])
        wait_bytes(o_recv.at[h, pl.ds(0, nx - 1)], o_sem_s.at[h])
        wait_bytes(at.at[h, pl.ds(0, ny - 1)], y_sem_s.at[h])


def shards(
    nx,
    queries,
    new_keys,
    new_values,
    residual,
    w_out,
    leaf_keys,
    leaf_values,
    upper_keys,
    upper_values,
    req_len,
    leaf_mid,
    mid_root,
    upper_len,
    leaf_len,
):
    ny = lax.axis_size("grp")
    nz = lax.axis_size("tok") // (nx * CORES)
    rows, width = queries.shape
    heads = width // HEAD_DIM
    nodes, depth, _ = upper_keys.shape
    leaf_pos = leaf_keys.shape[1]
    roots = nodes - mid_root.shape[0]
    stat_width = -(-rows // 128) * 128
    bf16, f32 = jnp.bfloat16, jnp.float32
    dma = pltpu.SemaphoreType.DMA
    scratch = [pltpu.VMEM((2, nz, nodes, 16, HEAD_DIM), bf16) for _ in range(heads)]
    scratch += [
        pltpu.VMEM((2, nodes * depth, width), bf16),
        pltpu.VMEM((nodes * depth, width), bf16),
        pltpu.VMEM((nx, rows, width), bf16),
        pltpu.VMEM((leaf_pos, width), bf16),
        pltpu.VMEM((leaf_pos, width), bf16),
        pltpu.VMEM((rows, width), bf16),
        pltpu.VMEM((rows, width), bf16),
        pltpu.VMEM((rows, width), bf16),
        pltpu.VMEM((ny, width, width), bf16),
        pltpu.VMEM((heads, rows, HEAD_DIM), f32),
        pltpu.VMEM((heads, rows, HEAD_DIM), f32),
        pltpu.VMEM((heads, nx, rows, HEAD_DIM), bf16),
        pltpu.VMEM((heads, nx, rows, HEAD_DIM), bf16),
        pltpu.VMEM((heads, nx, 8, stat_width), f32),
        pltpu.VMEM((heads, nx, 8, stat_width), f32),
        pltpu.VMEM((heads, ny, rows, HEAD_DIM), bf16),
        pltpu.VMEM((rows, width), f32),
        dma((9,)),
        dma((2,)),
        dma((heads,)),
        dma((heads, 2, nz // 2)),
        dma((heads,)),
        dma((heads,)),
        dma((2,)),
        dma((2,)),
        dma((2,)),
        dma((heads,)),
        dma((heads,)),
        dma((heads,)),
        dma((heads,)),
        dma((heads,)),
        dma((heads,)),
    ]
    smem = pl.BlockSpec(memory_space=pltpu.SMEM)
    anyspace = pl.BlockSpec(memory_space=pl.ANY)
    return pl.pallas_call(
        functools.partial(kernel, nx, nz, ny, heads, roots),
        out_shape=jax.ShapeDtypeStruct((rows, width), bf16),
        in_specs=[smem] * 5 + [anyspace] * 9,
        out_specs=pl.BlockSpec(memory_space=pltpu.VMEM),
        scratch_shapes=scratch,
        compiler_params=pltpu.CompilerParams(
            collective_id=0, has_side_effects=True, vmem_limit_bytes=40 * 1024 * 1024
        ),
    )(
        req_len,
        leaf_mid,
        mid_root,
        upper_len,
        leaf_len,
        upper_keys.reshape(nodes * depth, width),
        upper_values.reshape(nodes * depth, width),
        queries,
        new_keys,
        new_values,
        residual,
        w_out,
        leaf_keys.reshape(leaf_pos, width),
        leaf_values.reshape(leaf_pos, width),
    )


def solution(mesh, nx=CHIPS_X):
    in_specs = (
        P("tok", "grp"),
        P("tok", "grp"),
        P("tok", "grp"),
        P("tok", "grp"),
        P("grp", None),
        P("tok", None, "grp"),
        P("tok", None, "grp"),
        P(None, "tok", "grp"),
        P(None, "tok", "grp"),
        P(),
        P(),
        P(),
        P(),
        P(),
    )
    return jax.shard_map(
        functools.partial(shards, nx),
        mesh=mesh,
        in_specs=in_specs,
        out_specs=P("tok", "grp"),
        check_vma=False,
    )
```

time: 359 us -> 78.8 us (0.22)
  the two profiles are of different devices: /device:TPU:1 before, /device:TPU:6 now
where the time goes in v1:
time: 78.8 us; the launch traced here: 78.3 us
  Pallas kernels  65.3 us (83%)
  local copies, waits for them, and re-layouts  12.9 us (16%)
    pallas_call x1, Pallas kernels, shards(): pl.pallas_call(functools.partial(kernel, nx, nz, ny, heads, roots), out_s...  65.3 us
    unnamed x29, local copies, waits for them, and re-layouts  12.9 us

profile of v1, /device:TPU:6, one launch (start us, length us, event | category | flops | bytes accessed | tf_op | source)
XLA Modules:
  0.0 78.3 jit_solution(7193964629500532860)
XLA Ops:
  0.0 0.0 copy-start
  0.0 1.6 %copy-done = bf16[512,2048]{1,0:T(8,128)(2,1)S(1)} copy-done((bf16[512,2048]{1,0:T(8,128)(2,1)S(1)}, bf16[512,2048]{1,0:T(8,128)(2,1)}, u32[]{:S(2)}) %copy-start) | copy-done | bytes 2097176
  1.6 0.0 copy-start.1
  1.6 1.0 %copy-done.1 = bf16[1,512,512]{2,1,0:T(8,128)(2,1)S(1)} copy-done((bf16[1,512,512]{2,1,0:T(8,128)(2,1)S(1)}, bf16[1,512,512]{2,1,0:T(8,128)(2,1)}, u32[]{:S(2)}) %copy-start.1) | copy-done | bytes 524312
  2.6 0.0 copy-start.2
  2.6 1.0 %copy-done.2 = bf16[1,512,512]{2,1,0:T(8,128)(2,1)S(1)} copy-done((bf16[1,512,512]{2,1,0:T(8,128)(2,1)S(1)}, bf16[1,512,512]{2,1,0:T(8,128)(2,1)}, u32[]{:S(2)}) %copy-start.2) | copy-done | bytes 524312
  3.7 0.0 copy-start.3
  3.7 0.9 %copy-done.3 = bf16[192,512]{1,0:T(8,128)(2,1)S(1)} copy-done((bf16[192,512]{1,0:T(8,128)(2,1)S(1)}, bf16[192,512]{1,0:T(8,128)(2,1)}, u32[]{:S(2)}) %copy-start.3) | copy-done | bytes 196632
  4.6 0.0 copy-start.4
  4.6 0.9 %copy-done.4 = bf16[192,512]{1,0:T(8,128)(2,1)S(1)} copy-done((bf16[192,512]{1,0:T(8,128)(2,1)S(1)}, bf16[192,512]{1,0:T(8,128)(2,1)}, u32[]{:S(2)}) %copy-start.4) | copy-done | bytes 196632
  5.5 0.0 copy-start.5
  5.5 0.9 %copy-done.5 = bf16[192,512]{1,0:T(8,128)(2,1)S(1)} copy-done((bf16[192,512]{1,0:T(8,128)(2,1)S(1)}, bf16[192,512]{1,0:T(8,128)(2,1)}, u32[]{:S(2)}) %copy-start.5) | copy-done | bytes 196632
  6.5 0.0 copy-start.6
  6.5 0.9 %copy-done.6 = bf16[192,512]{1,0:T(8,128)(2,1)S(1)} copy-done((bf16[192,512]{1,0:T(8,128)(2,1)S(1)}, bf16[192,512]{1,0:T(8,128)(2,1)}, u32[]{:S(2)}) %copy-start.6) | copy-done | bytes 196632
  7.4 0.0 copy-start.7
  7.4 0.8 %copy-done.7 = bf16[6,8,512]{2,1,0:T(8,128)(2,1)S(1)} copy-done((bf16[6,8,512]{2,1,0:T(8,128)(2,1)S(1)}, bf16[6,8,512]{2,1,0:T(8,128)(2,1)}, u32[]{:S(2)}) %copy-start.7) | copy-done | bytes 49176
  8.2 0.0 copy-start.8
  8.2 0.8 %copy-done.8 = bf16[6,8,512]{2,1,0:T(8,128)(2,1)S(1)} copy-done((bf16[6,8,512]{2,1,0:T(8,128)(2,1)S(1)}, bf16[6,8,512]{2,1,0:T(8,128)(2,1)}, u32[]{:S(2)}) %copy-start.8) | copy-done | bytes 49176
  9.0 0.0 copy-start.9
  9.0 0.7 copy-done.9
  9.6 0.0 copy-start.10
  9.6 0.7 copy-done.10
  10.3 0.0 copy-start.11
  10.3 0.7 copy-done.11
  11.0 0.0 copy-start.12
  11.0 0.7 copy-done.12
  11.6 0.0 copy-start.13
  11.6 0.7 copy-done.13
  12.3 65.3 %shard_map.136 = bf16[192,512]{1,0:T(8,128)(2,1)S(1)} custom-call(s32[128]{0:T(128)S(1)} %copy-done.9, s32[128]{0:T(128)S(1)} %copy-done.10, s32[4]{0:T(128)S(1)} %copy-done.11, s32[6]{0:T(128)S(1)} %copy-done.12, s32[128]{0:T(128)S(1)} %copy-done.13, bf16[48,512]{1,0:T(8,128)(2,1)S(1)} %bitcast.6, bf16[48,512]{1,0:T(8,128)(2,1)S(1)} %bitcast.7, ...), custom_call_target="tpu_custom_call" | custom-call | tf_op jit(solution)/shard_map/pallas_call | solution.py:443
  77.6 0.7 copy.16
Async XLA Ops:
  0.0 1.6 %copy-start = (bf16[512,2048]{1,0:T(8,128)(2,1)S(1)}, bf16[512,2048]{1,0:T(8,128)(2,1)}, u32[]{:S(2)}) copy-start(bf16[512,2048]{1,0:T(8,128)(2,1)} %w_hbm.1) | copy-start | bytes 6291460
  1.6 1.0 %copy-start.1 = (bf16[1,512,512]{2,1,0:T(8,128)(2,1)S(1)}, bf16[1,512,512]{2,1,0:T(8,128)(2,1)}, u32[]{:S(2)}) copy-start(bf16[1,512,512]{2,1,0:T(8,128)(2,1)} %param.19) | copy-start | bytes 1572868
  2.6 1.0 %copy-start.2 = (bf16[1,512,512]{2,1,0:T(8,128)(2,1)S(1)}, bf16[1,512,512]{2,1,0:T(8,128)(2,1)}, u32[]{:S(2)}) copy-start(bf16[1,512,512]{2,1,0:T(8,128)(2,1)} %param.20) | copy-start | bytes 1572868
  3.7 0.9 %copy-start.3 = (bf16[192,512]{1,0:T(8,128)(2,1)S(1)}, bf16[192,512]{1,0:T(8,128)(2,1)}, u32[]{:S(2)}) copy-start(bf16[192,512]{1,0:T(8,128)(2,1)} %q_hbm.1) | copy-start | bytes 589828
  4.6 0.9 %copy-start.4 = (bf16[192,512]{1,0:T(8,128)(2,1)S(1)}, bf16[192,512]{1,0:T(8,128)(2,1)}, u32[]{:S(2)}) copy-start(bf16[192,512]{1,0:T(8,128)(2,1)} %nk_hbm.1) | copy-start | bytes 589828
  5.5 0.9 %copy-start.5 = (bf16[192,512]{1,0:T(8,128)(2,1)S(1)}, bf16[192,512]{1,0:T(8,128)(2,1)}, u32[]{:S(2)}) copy-start(bf16[192,512]{1,0:T(8,128)(2,1)} %nv_hbm.1) | copy-start | bytes 589828
  6.5 0.9 %copy-start.6 = (bf16[192,512]{1,0:T(8,128)(2,1)S(1)}, bf16[192,512]{1,0:T(8,128)(2,1)}, u32[]{:S(2)}) copy-start(bf16[192,512]{1,0:T(8,128)(2,1)} %res_hbm.1) | copy-start | bytes 589828
  7.4 0.8 %copy-start.7 = (bf16[6,8,512]{2,1,0:T(8,128)(2,1)S(1)}, bf16[6,8,512]{2,1,0:T(8,128)(2,1)}, u32[]{:S(2)}) copy-start(bf16[6,8,512]{2,1,0:T(8,128)(2,1)} %param.21) | copy-start | bytes 147460
  8.2 0.8 %copy-start.8 = (bf16[6,8,512]{2,1,0:T(8,128)(2,1)S(1)}, bf16[6,8,512]{2,1,0:T(8,128)(2,1)}, u32[]{:S(2)}) copy-start(bf16[6,8,512]{2,1,0:T(8,128)(2,1)} %param.22) | copy-start | bytes 147460
  9.0 0.7 copy-start.9
  9.6 0.7 copy-start.10
  10.3 0.7 copy-start.11
  11.0 0.7 copy-start.12
  11.6 0.7 copy-start.13

commit v2 on v1

--- a/solution.py
+++ b/solution.py
@@ -12,6 +12,7 @@
 LOG2E = 1.4426950408889634
 CHIPS_X = 4
 CORES = 2
+SKEW = 0.5
 MESH = pl.DeviceIdType.MESH
 
 
@@ -69,11 +70,11 @@
     ny,
     heads,
     roots,
-    req_len,
-    leaf_mid,
-    mid_root,
-    upper_len,
-    leaf_len,
+    req_len_hbm,
+    leaf_mid_hbm,
+    mid_root_hbm,
+    upper_len_hbm,
+    leaf_len_hbm,
     uk,
     uv,
     q_hbm,
@@ -88,6 +89,11 @@
 ):
     kv = scratch[:heads]
     (
+        req_len,
+        leaf_mid,
+        mid_root,
+        upper_len,
+        leaf_len,
         up,
         up_other,
         qx,
@@ -134,8 +140,9 @@
         return ((z_ * nx + x_) * CORES + c_, y_)
 
     sibling = dev(z, x, 1 - c, y)
-    right = dev(lax.rem(z + 1, nz), x, c, y)
-    left = dev(lax.rem(z + nz - 1, nz), x, c, y)
+
+    def z_mate(hops):
+        return dev(lax.rem(z + nz + hops, nz), x, c, y)
 
     def x_mate(k):
         return lax.rem(x + k, nx)
@@ -153,12 +160,17 @@
         (nv_hbm, nv),
         (res_hbm, res),
         (w_hbm.at[:, pl.ds(pl.multiple_of(y * width, width), width)], w.at[y]),
+        (req_len_hbm, req_len),
+        (leaf_mid_hbm, leaf_mid),
+        (mid_root_hbm, mid_root),
+        (upper_len_hbm, upper_len),
+        (leaf_len_hbm, leaf_len),
     ]
     loads = [pltpu.make_async_copy(a, b, in_sem.at[i]) for i, (a, b) in enumerate(loads)]
     for load in loads:
         load.start()
 
-    partners = [sibling, right, left]
+    partners = [sibling] + [z_mate(hops) for hops in (1, -1, 2, -2)]
     partners += [dev(z, x_mate(k), c, y) for k in range(1, nx)]
     partners += [dev(z, x, c, y_mate(k)) for k in range(1, ny)]
     barrier = pltpu.get_barrier_semaphore()
@@ -200,43 +212,62 @@
     for h in range(heads):
         kv[h][c, z] = block[:, :, h * HEAD_DIM : (h + 1) * HEAD_DIM]
 
-    steps = nz // 2
+    far = nz // 2
+    stages = -(-far // 2)
     cut = nodes // 2
 
-    def ring_view(h, direction, step):
-        slot = lax.rem(z + (nz - step if direction == 0 else step), nz)
-        view = kv[h].at[c, slot]
-        return view
-
-    def ring_part(h, direction, step, hop):
-        view = ring_view(h, direction, step)
-        if hop == steps:
+    def z_view(h, direction, distance):
+        return kv[h].at[c, lax.rem(z + (nz - distance if direction == 0 else distance), nz)]
+
+    def z_part(h, direction, held, distance):
+        view = z_view(h, direction, held)
+        if distance == far:
             view = view.at[pl.ds(0, cut)] if direction == 0 else view.at[pl.ds(cut, nodes - cut)]
         return view
 
-    def ring_start(h, direction, step):
-        view = ring_part(h, direction, step, step + 1)
-        send(
-            view,
-            view,
-            ring_send.at[h],
-            ring_recv.at[h, direction, step],
-            right if direction == 0 else left,
-        )
-
-    def ring_wait(h, direction, step):
+    def z_start(h, stage):
+        for hops in (2, 1):
+            for direction in range(2):
+                distance = 2 * stage + hops
+                if distance <= far:
+                    view = z_part(h, direction, 2 * stage, distance)
+                    send(
+                        view,
+                        view,
+                        ring_send.at[h],
+                        ring_recv.at[h, direction, distance - 1],
+                        z_mate(hops if direction == 0 else -hops),
+                    )
+
+    def z_wait(h, direction, distance):
         wait_bytes(
-            ring_part(h, direction, step + 1, step + 1), ring_recv.at[h, direction, step]
+            z_part(h, direction, distance, distance), ring_recv.at[h, direction, distance - 1]
         )
 
     def share(h, view):
         send(view, view, sib_send.at[h], sib_recv.at[h], sibling)
 
-    for h in range(heads):
+    def z_stage(h, stage):
+        if stage == 0:
+            z_start(h, 0)
+            share(h, kv[h].at[c, z])
+            return
         for direction in range(2):
-            ring_start(h, direction, 0)
-    for h in range(heads):
-        share(h, kv[h].at[c, z])
+            z_wait(h, direction, 2 * stage)
+        z_start(h, stage)
+        for direction in range(2):
+            share(h, z_view(h, direction, 2 * stage))
+        for direction in range(2):
+            z_wait(h, direction, 2 * stage - 1)
+            share(h, z_view(h, direction, 2 * stage - 1))
+
+    def z_finish(h):
+        for distance in range(2 * stages - 1, far + 1):
+            for direction in range(2):
+                z_wait(h, direction, distance)
+                if distance < far:
+                    share(h, z_view(h, direction, distance))
+        share(h, z_view(h, 0, far))
 
     me = tok
     position = lax.broadcasted_iota(jnp.int32, (rows, 1), 0)
@@ -256,30 +287,17 @@
         leaf_o[h] = o
         leaf_lse[h] = jnp.broadcast_to(lse, (rows, HEAD_DIM))
 
-    for step in range(steps - 1):
-        for h in range(heads):
-            for direction in range(2):
-                ring_wait(h, direction, step)
-                ring_start(h, direction, step + 1)
-                share(h, ring_view(h, direction, step + 1))
-        if step == 0:
-            for load in loads[2:7]:
+    def leaf_head(h):
+        if h == 0:
+            for load in loads[2:7] + loads[9:]:
                 load.wait()
-            for h in range(max(0, heads - steps + 1)):
-                leaf_part(h)
-        h = step + max(0, heads - steps + 1)
-        if h < heads:
-            leaf_part(h)
-    for h in range(heads):
-        for direction in range(2):
-            ring_wait(h, direction, steps - 1)
-        share(h, ring_view(h, 0, steps))
-
-    wait_bytes(w.at[pl.ds(0, ny - 1), pl.ds(0, half_rows)], w_sem.at[1])
-    for k in range(1, ny):
-        view = w.at[y_mate(k), my_half]
-        send(view, view, wf_sem.at[0], wf_sem.at[1], sibling)
-    wait_bytes(qx.at[pl.ds(0, nx - 1)], q_sem.at[1])
+        leaf_part(h)
+
+    def share_w():
+        wait_bytes(w.at[pl.ds(0, ny - 1), pl.ds(0, half_rows)], w_sem.at[1])
+        for k in range(1, ny):
+            view = w.at[y_mate(k), my_half]
+            send(view, view, wf_sem.at[0], wf_sem.at[1], sibling)
 
     keys = nz * 16
 
@@ -304,6 +322,8 @@
         return o.astype(jnp.bfloat16), jnp.broadcast_to(row, (8, row.shape[1]))
 
     def upper_head(h):
+        if h == 0:
+            wait_bytes(qx.at[pl.ds(0, nx - 1)], q_sem.at[1])
         wait_bytes(kv[h].at[1 - c], sib_recv.at[h])
 
         @pl.loop(1, nx)
@@ -355,14 +375,19 @@
         else:
             out[...] = total.astype(out.dtype)
 
+    events = [(stages - 0.6, share_w)]
+    for h in range(heads):
+        for stage in range(stages):
+            events.append((stage + SKEW * h, functools.partial(z_stage, h, stage)))
+        end = stages + SKEW * h
+        events.append((0.6 + 0.5 * h, functools.partial(leaf_head, h)))
+        events.append((end, functools.partial(z_finish, h)))
+        events.append((end + 0.4, functools.partial(upper_head, h)))
+        events.append((end + 1.6, functools.partial(merge_head, h)))
+        events.append((end + 2.8, functools.partial(project_head, h)))
     loads[7].wait()
-    for i in range(heads + 2):
-        if i < heads:
-            upper_head(i)
-        if 1 <= i <= heads:
-            merge_head(i - 1)
-        if i >= 2:
-            project_head(i - 2)
+    for _, event in sorted(events, key=lambda item: item[0]):
+        event()
 
     wait_bytes(up_other, pre_sem.at[0])
     wait_bytes(qx.at[pl.ds(0, nx - 1)], q_sem.at[0])
@@ -404,6 +429,7 @@
     bf16, f32 = jnp.bfloat16, jnp.float32
     dma = pltpu.SemaphoreType.DMA
     scratch = [pltpu.VMEM((2, nz, nodes, 16, HEAD_DIM), bf16) for _ in range(heads)]
+    scratch += [pltpu.SMEM(a.shape, a.dtype) for a in (req_len, leaf_mid, mid_root, upper_len, leaf_len)]
     scratch += [
         pltpu.VMEM((2, nodes * depth, width), bf16),
         pltpu.VMEM((nodes * depth, width), bf16),
@@ -422,7 +448,7 @@
         pltpu.VMEM((heads, nx, 8, stat_width), f32),
         pltpu.VMEM((heads, ny, rows, HEAD_DIM), bf16),
         pltpu.VMEM((rows, width), f32),
-        dma((9,)),
+        dma((14,)),
         dma((2,)),
         dma((heads,)),
         dma((heads, 2, nz // 2)),
@@ -438,16 +464,15 @@
         dma((heads,)),
         dma((heads,)),
     ]
-    smem = pl.BlockSpec(memory_space=pltpu.SMEM)
-    anyspace = pl.BlockSpec(memory_space=pl.ANY)
+    hbm = pl.BlockSpec(memory_space=pltpu.HBM)
     return pl.pallas_call(
         functools.partial(kernel, nx, nz, ny, heads, roots),
         out_shape=jax.ShapeDtypeStruct((rows, width), bf16),
-        in_specs=[smem] * 5 + [anyspace] * 9,
+        in_specs=[hbm] * 14,
         out_specs=pl.BlockSpec(memory_space=pltpu.VMEM),
         scratch_shapes=scratch,
         compiler_params=pltpu.CompilerParams(
-            collective_id=0, has_side_effects=True, vmem_limit_bytes=40 * 1024 * 1024
+            collective_id=0, has_side_effects=True, vmem_limit_bytes=63 * 1024 * 1024
         ),
     )(
         req_len,

time: 78.8 us -> 59.2 us (0.75)
  the two profiles are of different devices: /device:TPU:6 before, /device:TPU:1 now
where the time goes in v2:
time: 59.2 us; the launch traced here: 59 us
  Pallas kernels  57.4 us (97%)
  local copies, waits for them, and re-layouts  1.62 us (3%)
    pallas_call x1, Pallas kernels, shards(): pl.pallas_call(functools.partial(kernel, nx, nz, ny, heads, roots), out_s...  57.4 us
    unnamed x1, local copies, waits for them, and re-layouts  1.62 us

profile of v2, /device:TPU:1, one launch (start us, length us, event | category | flops | bytes accessed | tf_op | source)
XLA Modules:
  0.0 59.0 jit_solution(5843059440727235321)
XLA Ops:
  0.0 57.4 %shard_map.136 = bf16[192,512]{1,0:T(8,128)(2,1)} custom-call(s32[128]{0:T(128)} %req_len_hbm.1, s32[128]{0:T(128)} %leaf_mid_hbm.1, s32[4]{0:T(128)} %mid_root_hbm.1, s32[6]{0:T(128)} %upper_len_hbm.1, s32[128]{0:T(128)} %leaf_len_hbm.1, bf16[48,512]{1,0:T(8,128)(2,1)} %bitcast.6, bf16[48,512]{1,0:T(8,128)(2,1)} %bitcast.7, bf16[192,512]{1,0:T(8,128)(2,1)} %q_hbm.1, ...), custom_call_target="tpu_custom_call" | custom-call | tf_op jit(solution)/shard_map/pallas_call | solution.py:468
  57.4 1.6 %copy.16 = bf16[192,512]{1,0:T(8,128)(2,1)} copy(bf16[192,512]{1,0:T(8,128)(2,1)} %shard_map.136) | data formatting | bytes 393216

commit v3 on v2

--- a/solution.py
+++ b/solution.py
@@ -12,7 +12,10 @@
 LOG2E = 1.4426950408889634
 CHIPS_X = 4
 CORES = 2
-SKEW = 0.5
+OFFSETS = (0, 0.7, 1.4, 2.1)
+Q_AT, W_FROM = 0.02, 1.6
+Z_SKIPS = (4, 4, 4, 4)
+W_AT, UPPER_AT, MERGE_AT, PROJECT_AT = 3.4, 0.4, 1.6, 2.8
 MESH = pl.DeviceIdType.MESH
 
 
@@ -47,6 +50,15 @@
         spread = jnp.broadcast_to(row[:, start : start + 128], (n, 128))
         pieces.append(jnp.sum(jnp.where(diag, spread, 0.0), axis=1, keepdims=True))
     return jnp.concatenate(pieces, axis=0)
+
+
+def z_plan(far, skips):
+    plan, held = [], 0
+    while held < far:
+        hops = 2 if len(plan) < skips and held + 2 <= far else 1
+        plan.append([(held, n) for n in range(hops, 0, -1)])
+        held += hops
+    return plan
 
 
 def softmax_part(parts):
@@ -70,6 +82,7 @@
     ny,
     heads,
     roots,
+    z_skips,
     req_len_hbm,
     leaf_mid_hbm,
     mid_root_hbm,
@@ -95,7 +108,6 @@
         upper_len,
         leaf_len,
         up,
-        up_other,
         qx,
         lk,
         lv,
@@ -112,7 +124,6 @@
         at,
         acc,
         in_sem,
-        pre_sem,
         ring_send,
         ring_recv,
         sib_send,
@@ -176,6 +187,13 @@
     barrier = pltpu.get_barrier_semaphore()
     for partner in partners:
         pl.semaphore_signal(barrier, inc=1, device_id=partner, device_id_type=MESH)
+    loads[0].wait()
+    loads[1].wait()
+    block = jnp.concatenate(
+        [up[i].astype(jnp.float32).reshape(nodes, 8, width) for i in range(2)], axis=1
+    ).astype(jnp.bfloat16)
+    for h in range(heads):
+        kv[h][c, z] = block[:, :, h * HEAD_DIM : (h + 1) * HEAD_DIM]
     pl.semaphore_wait(barrier, len(partners))
 
     def send(src, dst, send_sem, recv_sem, device):
@@ -188,32 +206,24 @@
             device_id_type=MESH,
         ).start()
 
-    loads[0].wait()
-    loads[1].wait()
-    send(up.at[1 - c], up_other, pre_sem.at[0], pre_sem.at[1], sibling)
-    for k in range(1, nx):
-        send(q_hbm, qx.at[x], q_sem.at[0], q_sem.at[1], dev(z, x_mate(k), c, y))
     my_half = pl.ds(pl.multiple_of(c * half_rows, half_rows), half_rows)
-    for k in range(1, ny):
-        to = y_mate(k)
-        send(
-            w_hbm.at[my_half, pl.ds(pl.multiple_of(to * width, width), width)],
-            w.at[y, my_half],
-            w_sem.at[0],
-            w_sem.at[1],
-            dev(z, x, c, to),
-        )
-    wait_bytes(up_other, pre_sem.at[1])
-    mine = up[c].astype(jnp.float32).reshape(nodes, 8, width)
-    other = up_other[...].astype(jnp.float32).reshape(nodes, 8, width)
-    first = jnp.where(c == 0, mine, other)
-    second = jnp.where(c == 0, other, mine)
-    block = jnp.concatenate([first, second], axis=1).astype(jnp.bfloat16)
-    for h in range(heads):
-        kv[h][c, z] = block[:, :, h * HEAD_DIM : (h + 1) * HEAD_DIM]
+
+    def send_queries():
+        for k in sorted(range(1, nx), key=lambda k: -min(k, nx - k)):
+            send(q_hbm, qx.at[x], q_sem.at[0], q_sem.at[1], dev(z, x_mate(k), c, y))
+
+    def send_w():
+        for k in range(1, ny):
+            to = y_mate(k)
+            send(
+                w_hbm.at[my_half, pl.ds(pl.multiple_of(to * width, width), width)],
+                w.at[y, my_half],
+                w_sem.at[0],
+                w_sem.at[1],
+                dev(z, x, c, to),
+            )
 
     far = nz // 2
-    stages = -(-far // 2)
     cut = nodes // 2
 
     def z_view(h, direction, distance):
@@ -225,20 +235,6 @@
             view = view.at[pl.ds(0, cut)] if direction == 0 else view.at[pl.ds(cut, nodes - cut)]
         return view
 
-    def z_start(h, stage):
-        for hops in (2, 1):
-            for direction in range(2):
-                distance = 2 * stage + hops
-                if distance <= far:
-                    view = z_part(h, direction, 2 * stage, distance)
-                    send(
-                        view,
-                        view,
-                        ring_send.at[h],
-                        ring_recv.at[h, direction, distance - 1],
-                        z_mate(hops if direction == 0 else -hops),
-                    )
-
     def z_wait(h, direction, distance):
         wait_bytes(
             z_part(h, direction, distance, distance), ring_recv.at[h, direction, distance - 1]
@@ -247,27 +243,36 @@
     def share(h, view):
         send(view, view, sib_send.at[h], sib_recv.at[h], sibling)
 
+    plans = [z_plan(far, z_skips[min(h, len(z_skips) - 1)]) for h in range(heads)]
+
     def z_stage(h, stage):
-        if stage == 0:
-            z_start(h, 0)
-            share(h, kv[h].at[c, z])
-            return
-        for direction in range(2):
-            z_wait(h, direction, 2 * stage)
-        z_start(h, stage)
-        for direction in range(2):
-            share(h, z_view(h, direction, 2 * stage))
-        for direction in range(2):
-            z_wait(h, direction, 2 * stage - 1)
-            share(h, z_view(h, direction, 2 * stage - 1))
-
-    def z_finish(h):
-        for distance in range(2 * stages - 1, far + 1):
+        came = [0] if stage == 0 else [held + hops for held, hops in plans[h][stage - 1]]
+        go_on = sorted({held for held, _ in plans[h][stage]}) if stage < len(plans[h]) else []
+        for held in go_on:
+            if held:
+                for direction in range(2):
+                    z_wait(h, direction, held)
+        for held, hops in plans[h][stage] if stage < len(plans[h]) else ():
             for direction in range(2):
-                z_wait(h, direction, distance)
+                view = z_part(h, direction, held, held + hops)
+                send(
+                    view,
+                    view,
+                    ring_send.at[h],
+                    ring_recv.at[h, direction, held + hops - 1],
+                    z_mate(hops if direction == 0 else -hops),
+                )
+        for distance in sorted(came, key=lambda d: d not in go_on):
+            if distance == 0:
+                share(h, kv[h].at[c, z])
+                continue
+            for direction in range(2):
+                if distance not in go_on:
+                    z_wait(h, direction, distance)
                 if distance < far:
                     share(h, z_view(h, direction, distance))
-        share(h, z_view(h, 0, far))
+            if distance == far:
+                share(h, z_view(h, 0, far))
 
     me = tok
     position = lax.broadcasted_iota(jnp.int32, (rows, 1), 0)
@@ -306,18 +311,25 @@
         mid = leaf_mid[request]
         root = mid_root[mid]
         query = qx[j, :, h * HEAD_DIM : (h + 1) * HEAD_DIM]
-        root_scores = dot_nt(query, kv[h][0, :, root].reshape(keys, HEAD_DIM))
-        mid_scores = dot_nt(query, kv[h][0, :, roots + mid].reshape(keys, HEAD_DIM))
+
+        def rows_of(node):
+            both = kv[h][:, :, node].astype(jnp.float32).reshape(keys // 8, 16, HEAD_DIM)
+            return (
+                both[:, :8].reshape(keys, HEAD_DIM).astype(jnp.bfloat16),
+                both[:, 8:].reshape(keys, HEAD_DIM).astype(jnp.bfloat16),
+            )
+
+        root_keys, root_values = rows_of(root)
+        mid_keys, mid_values = rows_of(roots + mid)
+        root_scores = dot_nt(query, root_keys)
+        mid_scores = dot_nt(query, mid_keys)
         key = lax.broadcasted_iota(jnp.int32, mid_scores.shape, 1)
-        key_pos = (key >> 4) * (nx * 16) + (key & 15) + x * 16
+        core = (key >= keys // 2).astype(jnp.int32)
+        key = key - core * (keys // 2)
+        key_pos = (key >> 3) * (nx * 16) + x * 16 + core * 8 + (key & 7)
         root_scores = jnp.where(key_pos < upper_len[root], root_scores, NEG_FILL)
         mid_scores = jnp.where(key_pos < upper_len[roots + mid], mid_scores, NEG_FILL)
-        o, lse = softmax_part(
-            [
-                (root_scores, kv[h][1, :, root].reshape(keys, HEAD_DIM)),
-                (mid_scores, kv[h][1, :, roots + mid].reshape(keys, HEAD_DIM)),
-            ]
-        )
+        o, lse = softmax_part([(root_scores, root_values), (mid_scores, mid_values)])
         row = col_to_row(lse)
         return o.astype(jnp.bfloat16), jnp.broadcast_to(row, (8, row.shape[1]))
 
@@ -326,9 +338,9 @@
             wait_bytes(qx.at[pl.ds(0, nx - 1)], q_sem.at[1])
         wait_bytes(kv[h].at[1 - c], sib_recv.at[h])
 
-        @pl.loop(1, nx)
+        @pl.loop(0, nx - 1)
         def _(k):
-            j = lax.rem(x + k, nx)
+            j = lax.rem(x + lax.rem(k + nx // 2 - 1, nx - 1) + 1, nx)
             o, lse = upper_part(h, j)
             o_send[h, j] = o
             s_send[h, j] = lse
@@ -354,7 +366,7 @@
             weighted = weighted + weight * part
         attended = jnp.where(position < req_len[me], weighted / total, 0.0)
         at[h, y] = attended.astype(jnp.bfloat16)
-        for k in range(1, ny):
+        for k in sorted(range(1, ny), key=lambda k: -min(k, ny - k)):
             view = at.at[h, y]
             send(view, view, y_sem_s.at[h], y_sem_r.at[h], dev(z, x, c, y_mate(k)))
 
@@ -375,21 +387,19 @@
         else:
             out[...] = total.astype(out.dtype)
 
-    events = [(stages - 0.6, share_w)]
+    events = [(Q_AT, send_queries), (W_FROM, send_w), (W_AT, share_w)]
     for h in range(heads):
-        for stage in range(stages):
-            events.append((stage + SKEW * h, functools.partial(z_stage, h, stage)))
-        end = stages + SKEW * h
+        for stage in range(len(plans[h]) + 1):
+            events.append((stage + OFFSETS[h], functools.partial(z_stage, h, stage)))
+        end = len(plans[h]) + OFFSETS[h]
         events.append((0.6 + 0.5 * h, functools.partial(leaf_head, h)))
-        events.append((end, functools.partial(z_finish, h)))
-        events.append((end + 0.4, functools.partial(upper_head, h)))
-        events.append((end + 1.6, functools.partial(merge_head, h)))
-        events.append((end + 2.8, functools.partial(project_head, h)))
+        events.append((end + UPPER_AT, functools.partial(upper_head, h)))
+        events.append((end + MERGE_AT, functools.partial(merge_head, h)))
+        events.append((end + PROJECT_AT, functools.partial(project_head, h)))
     loads[7].wait()
     for _, event in sorted(events, key=lambda item: item[0]):
         event()
 
-    wait_bytes(up_other, pre_sem.at[0])
     wait_bytes(qx.at[pl.ds(0, nx - 1)], q_sem.at[0])
     wait_bytes(w.at[pl.ds(0, ny - 1), pl.ds(0, half_rows)], w_sem.at[0])
     wait_bytes(w.at[pl.ds(0, ny - 1), pl.ds(0, half_rows)], wf_sem.at[0])
@@ -432,7 +442,6 @@
     scratch += [pltpu.SMEM(a.shape, a.dtype) for a in (req_len, leaf_mid, mid_root, upper_len, leaf_len)]
     scratch += [
         pltpu.VMEM((2, nodes * depth, width), bf16),
-        pltpu.VMEM((nodes * depth, width), bf16),
         pltpu.VMEM((nx, rows, width), bf16),
         pltpu.VMEM((leaf_pos, width), bf16),
         pltpu.VMEM((leaf_pos, width), bf16),
@@ -449,7 +458,6 @@
         pltpu.VMEM((heads, ny, rows, HEAD_DIM), bf16),
         pltpu.VMEM((rows, width), f32),
         dma((14,)),
-        dma((2,)),
         dma((heads,)),
         dma((heads, 2, nz // 2)),
         dma((heads,)),
@@ -466,7 +474,7 @@
     ]
     hbm = pl.BlockSpec(memory_space=pltpu.HBM)
     return pl.pallas_call(
-        functools.partial(kernel, nx, nz, ny, heads, roots),
+        functools.partial(kernel, nx, nz, ny, heads, roots, Z_SKIPS),
         out_shape=jax.ShapeDtypeStruct((rows, width), bf16),
         in_specs=[hbm] * 14,
         out_specs=pl.BlockSpec(memory_space=pltpu.VMEM),

time: 59.2 us -> 56.9 us (0.961)
  Pallas kernels: 57.4 us -> 55.1 us
    pallas_call x1, Pallas kernels: 57.4 us -> 55.1 us  [shards(): pl.pallas_call(functools.partial(kernel, nx, nz, ny, heads, roots, Z_SKIP...]
where the time goes in v3:
time: 56.9 us; the launch traced here: 56.7 us
  Pallas kernels  55.1 us (97%)
  local copies, waits for them, and re-layouts  1.62 us (3%)
    pallas_call x1, Pallas kernels, shards(): pl.pallas_call(functools.partial(kernel, nx, nz, ny, heads, roots, Z_SKIP...  55.1 us
    unnamed x1, local copies, waits for them, and re-layouts  1.62 us

profile of v3, /device:TPU:1, one launch (start us, length us, event | category | flops | bytes accessed | tf_op | source)
XLA Modules:
  0.0 56.7 jit_solution(4099756681281575934)
XLA Ops:
  0.0 55.1 %shard_map.136 = bf16[192,512]{1,0:T(8,128)(2,1)} custom-call(s32[128]{0:T(128)} %req_len_hbm.1, s32[128]{0:T(128)} %leaf_mid_hbm.1, s32[4]{0:T(128)} %mid_root_hbm.1, s32[6]{0:T(128)} %upper_len_hbm.1, s32[128]{0:T(128)} %leaf_len_hbm.1, bf16[48,512]{1,0:T(8,128)(2,1)} %bitcast.6, bf16[48,512]{1,0:T(8,128)(2,1)} %bitcast.7, bf16[192,512]{1,0:T(8,128)(2,1)} %q_hbm.1, ...), custom_call_target="tpu_custom_call" | custom-call | tf_op jit(solution)/shard_map/pallas_call | solution.py:476
  55.1 1.6 %copy.16 = bf16[192,512]{1,0:T(8,128)(2,1)} copy(bf16[192,512]{1,0:T(8,128)(2,1)} %shard_map.136) | data formatting | bytes 393216

commit v4 on v3

--- a/solution.py
+++ b/solution.py
@@ -13,6 +13,7 @@
 CHIPS_X = 4
 CORES = 2
 OFFSETS = (0, 0.7, 1.4, 2.1)
+LEAF_AT = (0.75, 0.8, 0.85, 0.9)
 Q_AT, W_FROM = 0.02, 1.6
 Z_SKIPS = (4, 4, 4, 4)
 W_AT, UPPER_AT, MERGE_AT, PROJECT_AT = 3.4, 0.4, 1.6, 2.8
@@ -392,7 +393,7 @@
         for stage in range(len(plans[h]) + 1):
             events.append((stage + OFFSETS[h], functools.partial(z_stage, h, stage)))
         end = len(plans[h]) + OFFSETS[h]
-        events.append((0.6 + 0.5 * h, functools.partial(leaf_head, h)))
+        events.append((LEAF_AT[h], functools.partial(leaf_head, h)))
         events.append((end + UPPER_AT, functools.partial(upper_head, h)))
         events.append((end + MERGE_AT, functools.partial(merge_head, h)))
         events.append((end + PROJECT_AT, functools.partial(project_head, h)))

time: 56.9 us -> 57.3 us (level)
  no operation moved by 1% of the time
where the time goes in v4:
time: 57.3 us; the launch traced here: 57.2 us
  Pallas kernels  55.6 us (97%)
  local copies, waits for them, and re-layouts  1.62 us (3%)
    pallas_call x1, Pallas kernels, shards(): pl.pallas_call(functools.partial(kernel, nx, nz, ny, heads, roots, Z_SKIP...  55.6 us
    unnamed x1, local copies, waits for them, and re-layouts  1.62 us

profile of v4, /device:TPU:1, one launch (start us, length us, event | category | flops | bytes accessed | tf_op | source)
XLA Modules:
  0.0 57.2 jit_solution(13025871410375299508)
XLA Ops:
  0.0 55.6 %shard_map.136 = bf16[192,512]{1,0:T(8,128)(2,1)} custom-call(s32[128]{0:T(128)} %req_len_hbm.1, s32[128]{0:T(128)} %leaf_mid_hbm.1, s32[4]{0:T(128)} %mid_root_hbm.1, s32[6]{0:T(128)} %upper_len_hbm.1, s32[128]{0:T(128)} %leaf_len_hbm.1, bf16[48,512]{1,0:T(8,128)(2,1)} %bitcast.6, bf16[48,512]{1,0:T(8,128)(2,1)} %bitcast.7, bf16[192,512]{1,0:T(8,128)(2,1)} %q_hbm.1, ...), custom_call_target="tpu_custom_call" | custom-call | tf_op jit(solution)/shard_map/pallas_call | solution.py:477
  55.6 1.6 %copy.16 = bf16[192,512]{1,0:T(8,128)(2,1)} copy(bf16[192,512]{1,0:T(8,128)(2,1)} %shard_map.136) | data formatting | bytes 393216
